TPU v7x, 512 devices: a whole 4x8x8 slice. The times are simulated.
512 devices in a mesh: dom: 512 (over x, z, y, core).
Axes of the slice: x: 4, y: 8, z: 8, core: 2. Of those that a mesh axis runs over, the one named last changes fastest.
Arguments:
- right_side: float32 [131072, 256], P('dom'), may hold values from -100 to 100
- noise_precision: bfloat16 [131072, 256], P('dom'), may hold values from 0.19921875 to 2
- degree: float32 [131072], P('dom'), as said below
- dependence: float32 [], replicated, may hold values from 0.5 to 0.95
- var_precision: float32 [256, 256], replicated, may hold values from -1 to 3, as said below
- local_tiles: float32 [1024, 2, 128, 128], P('dom'), may hold values from 0 to 0.06, as said below
- tile_cols: int32 [1024, 2], P('dom'), may hold values from 0 to 1, as said below
- tile_count: int32 [1024], P('dom'), may hold values from 1 to 2, as said below
- halo_tile: int32 [512, 4], P('dom'), may hold values from 0 to 1
- send_rows: int32 [512, 4, 64], P('dom'), may hold values from 0 to 127, as said below
- send_count: int32 [512, 4], P('dom'), may hold values from 0 to 64, as said below
- halo_weights: float32 [512, 4, 64, 128], P('dom'), may hold values from 0 to 0.06, as said below
Outputs:
- solution: float32 [131072, 256], P('dom')
Inputs may be any that keep to these rules, and one draw needn't show every extreme that they name: `tile_cols`: for each row tile r, the first tile_count slots name distinct column tiles of the same partition in any order, one of them r itself; every named tile lies in r's aligned group of 2 row tiles; later slots name the other tiles of that group. `tile_count`: row tile s is named by row tile r exactly when r is named by s. Some row tile names 2 tiles. `local_tiles`: used slots hold the weights between the blocks of the row tile and of the named column tile; the tiles of the pairs (r, s) and (s, r) are transposes of each other, and no block is adjacent to itself. Unused slots hold arbitrary values. `send_rows`: for each partition and direction, the 64 slots name distinct blocks of that direction's border row tile. `send_count`: zero exactly where a partition has no neighbour in a direction, otherwise at least 16; some count equals 64. The weights are those of a symmetric W: for used slots, halo_weights[p, c, k, send_rows[p, c, l]] = halo_weights[q, c', l, send_rows[q, c', k]]; in a used slot, entries in blocks that are not among p's used send_rows of that direction are zero. Slots at or past the neighbour's send_count hold arbitrary values. `degree`: the sum of each block's row of W. `var_precision`: Symmetric.
All inputs are finite; a program needn't handle non-finite values.
Results may differ from a plain program's by a relative error of at most 0.0003.
Values sent between devices are 32-bit elements; how exact they have to be, the bound alone decides.
A program may use at most 64 MiB of HBM per device.

v0:
```python
import jax
import jax.numpy as jnp
from jax import lax
from jax.sharding import PartitionSpec as P

GRID_W = 16
ITERS = 3


highest_precision = lax.Precision.HIGHEST


def from_behind(block, axis, distance):
    devices = range(lax.axis_size(axis))
    route = [(i - distance, i) for i in devices if i - distance in devices]
    return lax.ppermute(block, axis, route)


def squared_total(vector):
    return lax.psum(jnp.sum(vector * vector), "dom")


def local(
    right_side,
    noise_precision,
    degree,
    dependence,
    var_precision,
    local_tiles,
    tile_cols,
    tile_count,
    halo_tile,
    send_rows,
    send_count,
    halo_weights,
):
    blocks_here, variables = right_side.shape
    tile_size = local_tiles.shape[2]
    row_count = blocks_here // tile_size
    slot_total = send_rows.shape[2]
    offsets = (1, -1, GRID_W, -GRID_W)
    reverse = (1, 0, 3, 2)
    noise_wide = noise_precision.astype(jnp.float32)
    border_rows = halo_tile[0]
    sent_count = send_count[0]
    sent_rows = send_rows[0]
    border_weights = halo_weights[0]
    in_use = (jnp.arange(slot_total)[None, :] < sent_count[:, None]).astype(jnp.float32)
    gather_index = border_rows[:, None] * tile_size + sent_rows
    solution = jnp.zeros_like(right_side)
    residual = right_side
    direction = right_side
    norm_now = squared_total(residual)
    for iteration in range(ITERS):
        within_as_tiles = direction.reshape(row_count, tile_size, variables)
        results = []
        for row_tile in range(row_count):

            def accumulate_submatrix(slot, running, row_tile=row_tile):
                weight_tile = lax.dynamic_index_in_dim(
                    local_tiles[row_tile], slot, 0, keepdims=False
                )
                column_tile = lax.dynamic_index_in_dim(
                    within_as_tiles, tile_cols[row_tile, slot], 0, keepdims=False
                )
                return running + jnp.dot(
                    weight_tile,
                    column_tile,
                    precision=highest_precision,
                    preferred_element_type=jnp.float32,
                )

            start = jnp.zeros((tile_size, variables), jnp.float32)
            results.append(lax.fori_loop(0, tile_count[row_tile], accumulate_submatrix, start))
        total = jnp.zeros((row_count, tile_size, variables), jnp.float32)
        outgoing = direction[gather_index] * in_use[:, :, None]
        for heading in range(4):
            arrived = from_behind(outgoing[reverse[heading]], "dom", -offsets[heading])
            contribution = jnp.einsum(
                "ka,kv->av", border_weights[heading], arrived, precision=highest_precision
            )
            total = total.at[border_rows[heading]].add(contribution)
        coupled = jnp.concatenate(results, 0) + total.reshape(blocks_here, variables)
        interim = degree[:, None] * direction - dependence * coupled
        image = (
            jnp.dot(
                interim,
                var_precision,
                precision=highest_precision,
                preferred_element_type=jnp.float32,
            )
            + noise_wide * direction
        )
        step_size = norm_now / lax.psum(jnp.sum(direction * image), "dom")
        solution = solution + step_size * direction
        residual = residual - step_size * image
        if iteration + 1 < ITERS:
            norm_next = squared_total(residual)
            direction = residual + norm_next / norm_now * direction
            norm_now = norm_next
    return solution


def solution(mesh):
    placed = (
        P("dom", None),
        P("dom", None),
        P("dom"),
        P(),
        P(),
        P("dom", None, None, None),
        P("dom", None),
        P("dom"),
        P("dom", None),
        P("dom", None, None),
        P("dom", None),
        P("dom", None, None, None),
    )
    return jax.shard_map(
        local, mesh=mesh, in_specs=placed, out_specs=P("dom", None), check_vma=False
    )
```

profile of v0, /device:TPU:1, one launch (start us, length us, event | category | flops | bytes accessed | tf_op | source)
XLA Modules:
  0.0 620.4 jit_solution(16163772067033734463)
XLA Ops:
  0.0 0.7 multiply_bitcast_fusion
  0.7 0.8 compare_select_fusion
  1.6 0.7 copy-done.8
  2.3 1.9 gather_fusion
  4.3 8.9 %collective-permute-start = (f32[64,256]{1,0:T(8,128)S(1)}, f32[64,256]{1,0:T(8,128)S(1)}, u32[]{:S(2)}, u32[]{:S(2)}) collective-permute-start(f32[64,256]{1,0:T(8,128)S(1)} %get-tuple-element.446), channel_id=1, source_target_pairs={{1,0},{2,1},{3,2},{4,3},{5,4},{6,5},{7,6},{8,7},{9,8},{10,9},{11,1... | collective-permute-start | bytes 196616 | tf_op jit(solution)/shard_map/ppermute | solution.py:16
  13.3 1.9 collective-permute-start.1
  15.2 1.3 collective-permute-start.2
  16.5 4.0 collective-permute-start.3
  20.5 0.7 fusion.118
  26.2 0.6 copy-done.7
  26.8 0.7 fusion.117
  27.5 0.6 copy-done.10
  28.2 4.2 while.72
  28.7 0.7 constant_dynamic-slice_fusion.12
  32.4 4.0 while.73
  33.1 0.6 constant_dynamic-slice_fusion.13
  39.5 0.6 copy-done.9
  40.1 0.8 and_reduce_fusion
  41.0 0.9 copy-done.4
  41.9 0.9 fusion.63
  42.8 1.0 fusion.57
  43.8 0.9 fusion.54
  44.7 1.0 fusion.51
  45.8 0.7 copy-done.5
  46.5 1.1 multiply_reduce_fusion.3
  47.6 113.0 %all-reduce = (f32[]{:T(128)}, f32[]{:T(128)}) all-reduce(f32[]{:T(128)} %get-tuple-element.354, f32[]{:T(128)} %get-tuple-element.353), channel_id=1, replica_groups=mesh['dom'=512] {'dom'}, use_global_device_ids=true, to_apply=%region_1.0 | all-reduce | flops 2 | bytes 16 | tf_op jit(solution)/shard_map/psum | solution.py:20
  161.9 0.7 multiply_reduce_fusion.2
  162.5 94.1 %psum.44 = f32[]{:T(128)} all-reduce(f32[]{:T(128)} %get-tuple-element.433), channel_id=1, replica_groups=mesh['dom'=512] {'dom'}, use_global_device_ids=true, to_apply=%region_13.14 | all-reduce | flops 1 | bytes 8 | tf_op jit(solution)/shard_map/psum | solution.py:20
  258.0 1.0 gather_fusion.1
  259.1 2.6 collective-permute-start.4
  261.6 3.0 collective-permute-start.5
  264.6 1.3 collective-permute-start.6
  265.9 4.0 collective-permute-start.7
  270.0 4.0 while.74
  270.5 0.6 constant_dynamic-slice_fusion.14
  273.1 0.3 convolution_add_fusion.17
  274.0 4.2 while.75
  274.7 0.6 constant_dynamic-slice_fusion.15
  277.2 0.3 convolution_add_fusion.18
  278.3 0.9 fusion.61
  279.2 1.0 fusion.48
  280.2 0.9 fusion.45
  281.1 1.0 fusion.42
  282.2 1.0 multiply_reduce_fusion.1
  283.2 106.5 %psum.45 = f32[]{:T(128)} all-reduce(f32[]{:T(128)} %get-tuple-element.456), channel_id=1, replica_groups=mesh['dom'=512] {'dom'}, use_global_device_ids=true, to_apply=%region_19.20 | all-reduce | flops 1 | bytes 8 | tf_op jit(solution)/shard_map/psum | solution.py:94
  391.0 0.7 multiply_reduce_fusion
  391.7 94.1 %psum.46 = f32[]{:T(128)} all-reduce(f32[]{:T(128)} %multiply_reduce_fusion), channel_id=1, replica_groups=mesh['dom'=512] {'dom'}, use_global_device_ids=true, to_apply=%region_21.22 | all-reduce | flops 1 | bytes 8 | tf_op jit(solution)/shard_map/psum | solution.py:20
  487.1 1.0 gather_fusion.2
  488.2 2.6 collective-permute-start.8
  490.8 3.0 collective-permute-start.9
  493.8 1.3 collective-permute-start.10
  495.1 4.0 collective-permute-start.11
  499.1 4.0 while.76
  499.7 0.6 constant_dynamic-slice_fusion.16
  502.2 0.3 convolution_add_fusion.19
  503.1 4.0 while.77
  503.8 0.6 constant_dynamic-slice_fusion.17
  507.1 0.9 fusion.59
  508.1 1.0 fusion.39
  509.1 0.9 fusion.36
  510.0 1.0 fusion.33
  511.0 1.0 fusion.64
  512.1 106.2 %psum.47 = f32[]{:T(128)} all-reduce(f32[]{:T(128)} %fusion.64), channel_id=1, replica_groups=mesh['dom'=512] {'dom'}, use_global_device_ids=true, to_apply=%region_27.28 | all-reduce | flops 1 | bytes 8 | tf_op jit(solution)/shard_map/psum | solution.py:94
  619.6 0.8 multiply_add_fusion
  (57 shorter events, 1.8 us)
Async XLA Ops:
  0.0 45.8 %copy-start = (f32[256,256]{1,0:T(8,128)S(1)}, f32[256,256]{1,0:T(8,128)}, u32[]{:S(2)}) copy-start(f32[256,256]{1,0:T(8,128)} %param.52) | copy-start | bytes 786436
  1.6 0.7 copy-start.8
  4.3 23.2 %copy-start.1 = (f32[256,256]{1,0:T(8,128)S(1)}, f32[256,256]{1,0:T(8,128)}, u32[]{:S(2)}) copy-start(f32[256,256]{1,0:T(8,128)} %param.48) | copy-start | bytes 786436
  4.3 23.2 %copy-start.2 = (f32[2,2,128,128]{3,2,1,0:T(8,128)S(1)}, f32[2,2,128,128]{3,2,1,0:T(8,128)}, u32[]{:S(2)}) copy-start(f32[2,2,128,128]{3,2,1,0:T(8,128)} %param.53) | copy-start | bytes 786436
  4.3 36.6 %collective-permute-start = (f32[64,256]{1,0:T(8,128)S(1)}, f32[64,256]{1,0:T(8,128)S(1)}, u32[]{:S(2)}, u32[]{:S(2)}) collective-permute-start(f32[64,256]{1,0:T(8,128)S(1)} %get-tuple-element.446), channel_id=1, source_target_pairs={{1,0},{2,1},{3,2},{4,3},{5,4},{6,5},{7,6},{8,7},{9,8},{10,9},{11,1... | collective-permute-start | bytes 196616 | tf_op jit(solution)/shard_map/ppermute | solution.py:16
  13.3 29.5 %collective-permute-start.1 = (f32[64,256]{1,0:T(8,128)S(1)}, f32[64,256]{1,0:T(8,128)S(1)}, u32[]{:S(2)}, u32[]{:S(2)}) collective-permute-start(f32[64,256]{1,0:T(8,128)S(1)} %get-tuple-element.445), channel_id=1, source_target_pairs={{0,1},{1,2},{2,3},{3,4},{4,5},{5,6},{6,7},{7,8},{8,9},{9,10},{10,1... | collective-permute-start | bytes 196616 | tf_op jit(solution)/shard_map/ppermute | solution.py:16
  15.2 5.3 copy-start.6
  15.2 28.6 %collective-permute-start.2 = (f32[64,256]{1,0:T(8,128)S(1)}, f32[64,256]{1,0:T(8,128)S(1)}, u32[]{:S(2)}, u32[]{:S(2)}) collective-permute-start(f32[64,256]{1,0:T(8,128)S(1)} %get-tuple-element.444), channel_id=1, source_target_pairs={{16,0},{17,1},{18,2},{19,3},{20,4},{21,5},{22,6},{23,7},{24,8},{25... | collective-permute-start | bytes 196616 | tf_op jit(solution)/shard_map/ppermute | solution.py:16
  16.5 28.2 %collective-permute-start.3 = (f32[64,256]{1,0:T(8,128)S(1)}, f32[64,256]{1,0:T(8,128)S(1)}, u32[]{:S(2)}, u32[]{:S(2)}) collective-permute-start(f32[64,256]{1,0:T(8,128)S(1)} %get-tuple-element.443), channel_id=1, source_target_pairs={{0,16},{1,17},{2,18},{3,19},{4,20},{5,21},{6,22},{7,23},{8,24},{9,... | collective-permute-start | bytes 196616 | tf_op jit(solution)/shard_map/ppermute | solution.py:16
  26.2 0.7 copy-start.7
  27.5 0.7 copy-start.10
  39.5 0.7 copy-start.9
  41.0 0.9 copy-start.4
  44.7 1.1 copy-start.3
  45.8 0.7 copy-start.5
  259.1 19.2 %collective-permute-start.4 = (f32[64,256]{1,0:T(8,128)S(1)}, f32[64,256]{1,0:T(8,128)S(1)}, u32[]{:S(2)}, u32[]{:S(2)}) collective-permute-start(f32[64,256]{1,0:T(8,128)S(1)} %get-tuple-element.442), channel_id=1, source_target_pairs={{1,0},{2,1},{3,2},{4,3},{5,4},{6,5},{7,6},{8,7},{9,8},{10,9},{11,1... | collective-permute-start | bytes 196616 | tf_op jit(solution)/shard_map/ppermute | solution.py:16
  261.6 17.6 %collective-permute-start.5 = (f32[64,256]{1,0:T(8,128)S(1)}, f32[64,256]{1,0:T(8,128)S(1)}, u32[]{:S(2)}, u32[]{:S(2)}) collective-permute-start(f32[64,256]{1,0:T(8,128)S(1)} %get-tuple-element.441), channel_id=1, source_target_pairs={{0,1},{1,2},{2,3},{3,4},{4,5},{5,6},{6,7},{7,8},{8,9},{9,10},{10,1... | collective-permute-start | bytes 196616 | tf_op jit(solution)/shard_map/ppermute | solution.py:16
  264.6 15.6 %collective-permute-start.6 = (f32[64,256]{1,0:T(8,128)S(1)}, f32[64,256]{1,0:T(8,128)S(1)}, u32[]{:S(2)}, u32[]{:S(2)}) collective-permute-start(f32[64,256]{1,0:T(8,128)S(1)} %get-tuple-element.440), channel_id=1, source_target_pairs={{16,0},{17,1},{18,2},{19,3},{20,4},{21,5},{22,6},{23,7},{24,8},{25... | collective-permute-start | bytes 196616 | tf_op jit(solution)/shard_map/ppermute | solution.py:16
  265.9 15.2 %collective-permute-start.7 = (f32[64,256]{1,0:T(8,128)S(1)}, f32[64,256]{1,0:T(8,128)S(1)}, u32[]{:S(2)}, u32[]{:S(2)}) collective-permute-start(f32[64,256]{1,0:T(8,128)S(1)} %get-tuple-element.439), channel_id=1, source_target_pairs={{0,16},{1,17},{2,18},{3,19},{4,20},{5,21},{6,22},{7,23},{8,24},{9,... | collective-permute-start | bytes 196616 | tf_op jit(solution)/shard_map/ppermute | solution.py:16
  488.2 18.9 %collective-permute-start.8 = (f32[64,256]{1,0:T(8,128)S(1)}, f32[64,256]{1,0:T(8,128)S(1)}, u32[]{:S(2)}, u32[]{:S(2)}) collective-permute-start(f32[64,256]{1,0:T(8,128)S(1)} %get-tuple-element.438), channel_id=1, source_target_pairs={{1,0},{2,1},{3,2},{4,3},{5,4},{6,5},{7,6},{8,7},{9,8},{10,9},{11,1... | collective-permute-start | bytes 196616 | tf_op jit(solution)/shard_map/ppermute | solution.py:16
  490.8 17.3 %collective-permute-start.9 = (f32[64,256]{1,0:T(8,128)S(1)}, f32[64,256]{1,0:T(8,128)S(1)}, u32[]{:S(2)}, u32[]{:S(2)}) collective-permute-start(f32[64,256]{1,0:T(8,128)S(1)} %get-tuple-element.437), channel_id=1, source_target_pairs={{0,1},{1,2},{2,3},{3,4},{4,5},{5,6},{6,7},{7,8},{8,9},{9,10},{10,1... | collective-permute-start | bytes 196616 | tf_op jit(solution)/shard_map/ppermute | solution.py:16
  493.8 15.3 %collective-permute-start.10 = (f32[64,256]{1,0:T(8,128)S(1)}, f32[64,256]{1,0:T(8,128)S(1)}, u32[]{:S(2)}, u32[]{:S(2)}) collective-permute-start(f32[64,256]{1,0:T(8,128)S(1)} %get-tuple-element.436), channel_id=1, source_target_pairs={{16,0},{17,1},{18,2},{19,3},{20,4},{21,5},{22,6},{23,7},{24,8},{25... | collective-permute-start | bytes 196616 | tf_op jit(solution)/shard_map/ppermute | solution.py:16
  495.1 14.9 %collective-permute-start.11 = (f32[64,256]{1,0:T(8,128)S(1)}, f32[64,256]{1,0:T(8,128)S(1)}, u32[]{:S(2)}, u32[]{:S(2)}) collective-permute-start(f32[64,256]{1,0:T(8,128)S(1)} %get-tuple-element.435), channel_id=1, source_target_pairs={{0,16},{1,17},{2,18},{3,19},{4,20},{5,21},{6,22},{7,23},{8,24},{9,... | collective-permute-start | bytes 196616 | tf_op jit(solution)/shard_map/ppermute | solution.py:16
where the time goes:
time: 622 us; the launch traced here: 620 us
  blocking collectives  514 us (83%)
  starting transfers between devices  37.8 us (6%)
  loops' own time  18.8 us (3%)
  matrix products  16.4 us (3%)
  between operations  15.2 us (2%)
  local copies, waits for them, and re-layouts  13.3 us (2%)
    psum x3, blocking collectives, squared_total(): return lax.psum(jnp.sum(vector * vector), 'dom')  301 us
    psum x2, blocking collectives, local(): step_size = norm_now / lax.psum(jnp.sum(direction * image), 'dom')  213 us
    ppermute x12, starting transfers between devices, from_behind(): return lax.ppermute(block, axis, route)  37.8 us
    another operation x6, loops' own time, local(): lax.fori_loop(0, tile_count[row_tile], accumulate_submatrix, start)  18.8 us
  transfers between devices with their start and end apart: 12, of which 0 were waited for; matrix products, arithmetic and copies ran while one was open for 3% of the time, Pallas kernels for 0%

commit v1 on v0

v1 whole, which is shorter than its diff:
```python
import functools

import jax
import jax.numpy as jnp
from jax import lax
from jax.experimental import pallas as pl
from jax.experimental.pallas import tpu as pltpu
from jax.sharding import PartitionSpec as P

MESH = pl.DeviceIdType.MESH
GRID_W = 16
ITERS = 3
OFFSETS = (1, -1, GRID_W, -GRID_W)
REVERSE = (1, 0, 3, 2)
STAGES = ((1, 16), (16, 8), (128, 4))
F32 = jnp.float32
BF16 = jnp.bfloat16


def split(value):
    high = value.astype(BF16)
    low = (value - high.astype(F32)).astype(BF16)
    return high, low


def as_left(value):
    high, low = split(value)
    return jnp.concatenate([high, low, high], axis=1)


def as_right(value):
    high, low = split(value)
    return jnp.concatenate([high, low, high], axis=0)


def keep_left(ref, value):
    high, low = split(value)
    n = value.shape[1]
    ref[:, 0:n] = high
    ref[:, n : 2 * n] = high
    ref[:, 2 * n : 3 * n] = low


def keep_right(ref, value):
    high, low = split(value)
    n = value.shape[0]
    ref[0:n, :] = high
    ref[n : 2 * n, :] = high
    ref[2 * n : 3 * n, :] = low


def dot(a, b):
    return jnp.dot(a, b, preferred_element_type=F32)


def fold(value):
    rows, lanes = value.shape
    tile = jnp.sum(value.reshape(rows // 8, 8, lanes), axis=0)
    tile = tile[:, 0:128] + tile[:, 128:256]
    return jnp.sum(tile, axis=0, keepdims=True)


def total_of(row):
    return jnp.sum(row, axis=1, keepdims=True)


def kernel(
    dependence_ref,
    tile_cols_ref,
    tile_count_ref,
    halo_tile_ref,
    send_count_ref,
    right_hbm,
    noise_hbm,
    degree_hbm,
    var_hbm,
    tiles_hbm,
    rows_hbm,
    halo_hbm,
    out_ref,
    right_ref,
    noise_ref,
    degree_ref,
    var_ref,
    tiles_ref,
    rows_ref,
    halo_ref,
    var_cat,
    local_cat,
    halo_cat,
    scatter,
    basis,
    sent,
    received,
    sums,
    load_sem,
    send_sem,
    recv_sem,
    sum_send_sem,
    sum_recv_sem,
):
    me = lax.axis_index("dom")
    loads = [
        pltpu.make_async_copy(src, dst, load_sem.at[i])
        for i, (src, dst) in enumerate(
            (
                (var_hbm, var_ref),
                (right_hbm, right_ref),
                (halo_hbm, halo_ref),
                (tiles_hbm, tiles_ref),
                (rows_hbm, rows_ref),
                (degree_hbm, degree_ref),
                (noise_hbm, noise_ref),
            )
        )
    ]
    for load in loads:
        load.start()

    column = lax.rem(me, GRID_W)
    line = me // GRID_W
    usable = (column < GRID_W - 1, column > 0, line < 512 // GRID_W - 1, line > 0)

    def partners(stride, size):
        place = lax.rem(me // stride, size)
        return [me + (lax.rem(place + j, size) - place) * stride for j in range(1, size)]

    barrier = pltpu.get_barrier_semaphore()
    greeted = 0
    for stride, size in STAGES:
        for partner in partners(stride, size):
            pl.semaphore_signal(barrier, inc=1, device_id=(partner,), device_id_type=MESH)
            greeted += 1
    for c in range(4):

        @pl.when(usable[c])
        def _():
            pl.semaphore_signal(barrier, inc=1, device_id=(me + OFFSETS[c],), device_id_type=MESH)

    for c in range(4):

        @pl.when(jnp.logical_not(usable[c]))
        def _():
            for k in range(ITERS):
                received[k, 64 * c : 64 * c + 64, :] = jnp.zeros((64, 256), F32)

    loads[0].wait()
    keep_right(var_cat, var_ref[...])
    loads[1].wait()
    loads[2].wait()
    for c in range(4):
        tile = halo_tile_ref[0, c]
        weights = halo_ref[0, c]
        block = jnp.concatenate(
            [jnp.where(tile == r, weights, jnp.zeros_like(weights)) for r in range(2)], axis=1
        )
        keep_left(halo_cat.at[64 * c : 64 * c + 64, :], block)

    field = right_ref[...]
    mapped = dot(as_left(field), var_cat[...])
    mapped_cat = as_right(mapped)
    outgoing = dot(halo_cat[...], mapped_cat)

    pl.semaphore_wait(barrier, greeted + sum(u.astype(jnp.int32) for u in usable))

    def copies(k):
        return [
            pltpu.make_async_remote_copy(
                src_ref=sent.at[k, 64 * c : 64 * c + 64, :],
                dst_ref=received.at[k, 64 * REVERSE[c] : 64 * REVERSE[c] + 64, :],
                send_sem=send_sem.at[k, c],
                recv_sem=recv_sem.at[k, REVERSE[c]],
                device_id=(me + OFFSETS[c],),
                device_id_type=MESH,
            )
            for c in range(4)
        ]

    def arrivals(k):
        return [
            pltpu.make_async_remote_copy(
                src_ref=sent.at[k, 64 * c : 64 * c + 64, :],
                dst_ref=received.at[k, 64 * c : 64 * c + 64, :],
                send_sem=send_sem.at[k, c],
                recv_sem=recv_sem.at[k, c],
                device_id=(me + OFFSETS[c],),
                device_id_type=MESH,
            )
            for c in range(4)
        ]

    def start(k, value):
        sent[k] = value
        for c in (2, 3, 0, 1):
            pl.when(usable[c])(copies(k)[c].start)

    def finish(k):
        for c in (0, 1, 2, 3):
            pl.when(usable[c])(arrivals(k)[c].wait_recv)

    start(0, outgoing)

    dependence = dependence_ref[0]
    loads[3].wait()
    loads[5].wait()
    on_diagonal = lax.broadcasted_iota(jnp.int32, (256, 256), 0) == lax.broadcasted_iota(
        jnp.int32, (256, 256), 1
    )
    diagonal = jnp.where(on_diagonal, degree_ref[...], 0.0)
    for r in range(2):
        row = []
        for s in range(2):
            block = jnp.zeros((128, 128), F32)
            for j in range(2):
                used = jnp.logical_and(tile_cols_ref[r, j] == s, tile_count_ref[r] > j)
                block = jnp.where(used, tiles_ref[r, j], block)
            row.append(block)
        block_row = diagonal[128 * r : 128 * r + 128] - dependence * jnp.concatenate(row, axis=1)
        keep_left(local_cat.at[128 * r : 128 * r + 128, :], block_row)
    loads[4].wait()
    places = []
    slot = lax.broadcasted_iota(jnp.int32, (1, 64), 1)
    for c in range(4):
        place = rows_ref[0, c : c + 1, :] + halo_tile_ref[0, c] * 128
        places.append(jnp.where(slot < send_count_ref[0, c], place, -1))
    places = jnp.concatenate(places, axis=1)
    hot = lax.broadcasted_iota(jnp.int32, (256, 256), 0) == places
    hot = jnp.where(hot, 1.0, 0.0).astype(BF16)
    scatter[:, 0:256] = hot
    scatter[:, 256:512] = hot
    loads[6].wait()

    moments = [fold(field * field)]
    basis[0] = field
    for k in range(ITERS):
        near = dot(local_cat[...], mapped_cat) + noise_ref[...].astype(F32) * field
        finish(k)
        far = dot(scatter[...], jnp.concatenate(split(received[k]), axis=0))
        image = near - dependence * far
        moments.append(fold(field * image))
        if k + 1 < ITERS:
            moments.append(fold(image * image))
            field = image
            basis[k + 1] = field
            mapped = dot(as_left(field), var_cat[...])
            mapped_cat = as_right(mapped)
            start(k + 1, dot(halo_cat[...], mapped_cat))

    sums[0, 0] = jnp.concatenate(moments + [jnp.zeros((2, 128), F32)], axis=0)
    pending = []
    for n, (stride, size) in enumerate(STAGES):
        moves = [
            pltpu.make_async_remote_copy(
                src_ref=sums.at[n, 0],
                dst_ref=sums.at[n, size - 1 - j],
                send_sem=sum_send_sem.at[n],
                recv_sem=sum_recv_sem.at[n],
                device_id=(partner,),
                device_id_type=MESH,
            )
            for j, partner in enumerate(partners(stride, size))
        ]
        for move in moves:
            move.start()
        whole = pltpu.make_async_remote_copy(
            src_ref=sums.at[n, 1:size],
            dst_ref=sums.at[n, 1:size],
            send_sem=sum_send_sem.at[n],
            recv_sem=sum_recv_sem.at[n],
            device_id=(me,),
            device_id_type=MESH,
        )
        whole.wait_recv()
        total = sums[n, 0]
        for j in range(1, size):
            total = total + sums[n, j]
        if n + 1 < len(STAGES):
            sums[n + 1, 0] = total
        pending.append(whole)

    m = [total[k : k + 1, :] for k in range(6)]
    rr0 = total_of(m[0])
    a0 = rr0 / total_of(m[1])
    rr1 = total_of(m[0] - 2.0 * a0 * m[1] + a0 * a0 * m[2])
    g0 = 1.0 + rr1 / rr0
    g1 = -a0
    a1 = rr1 / total_of(g0 * g0 * m[1] + 2.0 * g0 * g1 * m[2] + g1 * g1 * m[3])
    e1 = -a0 - a1 * g0
    e2 = -a1 * g1
    rr2 = total_of(
        m[0] + 2.0 * e1 * m[1] + (e1 * e1 + 2.0 * e2) * m[2] + 2.0 * e1 * e2 * m[3] + e2 * e2 * m[4]
    )
    b1 = rr2 / rr1
    f0 = 1.0 + b1 * g0
    f1 = e1 + b1 * g1
    f2 = e2
    a2 = rr2 / total_of(
        f0 * f0 * m[1]
        + 2.0 * f0 * f1 * m[2]
        + (f1 * f1 + 2.0 * f0 * f2) * m[3]
        + 2.0 * f1 * f2 * m[4]
        + f2 * f2 * m[5]
    )
    c0 = a0 + a1 * g0 + a2 * f0
    c1 = a1 * g1 + a2 * f1
    c2 = a2 * f2
    out_ref[...] = c0 * basis[0] + c1 * basis[1] + c2 * basis[2]

    for move in pending:
        move.wait_send()
    for k in range(ITERS):
        for c in range(4):
            pl.when(usable[c])(copies(k)[c].wait_send)


def local(
    right_side,
    noise_precision,
    degree,
    dependence,
    var_precision,
    local_tiles,
    tile_cols,
    tile_count,
    halo_tile,
    send_rows,
    send_count,
    halo_weights,
):
    smem = pl.BlockSpec(memory_space=pltpu.SMEM)
    hbm = pl.BlockSpec(memory_space=pl.ANY)
    return pl.pallas_call(
        kernel,
        out_shape=jax.ShapeDtypeStruct((256, 256), F32),
        in_specs=[smem] * 5 + [hbm] * 7,
        out_specs=pl.BlockSpec(memory_space=pltpu.VMEM),
        scratch_shapes=[
            pltpu.VMEM((256, 256), F32),
            pltpu.VMEM((256, 256), BF16),
            pltpu.VMEM((1, 256), F32),
            pltpu.VMEM((256, 256), F32),
            pltpu.VMEM((2, 2, 128, 128), F32),
            pltpu.VMEM((1, 4, 64), jnp.int32),
            pltpu.VMEM((1, 4, 64, 128), F32),
            pltpu.VMEM((768, 256), BF16),
            pltpu.VMEM((256, 768), BF16),
            pltpu.VMEM((256, 768), BF16),
            pltpu.VMEM((256, 512), BF16),
            pltpu.VMEM((ITERS, 256, 256), F32),
            pltpu.VMEM((ITERS, 256, 256), F32),
            pltpu.VMEM((ITERS, 256, 256), F32),
            pltpu.VMEM((len(STAGES), max(s for _, s in STAGES), 8, 128), F32),
            pltpu.SemaphoreType.DMA((7,)),
            pltpu.SemaphoreType.DMA((ITERS, 4)),
            pltpu.SemaphoreType.DMA((ITERS, 4)),
            pltpu.SemaphoreType.DMA((len(STAGES),)),
            pltpu.SemaphoreType.DMA((len(STAGES),)),
        ],
        compiler_params=pltpu.CompilerParams(
            collective_id=0, has_side_effects=True, vmem_limit_bytes=48 * 1024 * 1024
        ),
        name="conjugate_gradient",
    )(
        dependence.reshape(1),
        tile_cols,
        tile_count,
        halo_tile,
        send_count,
        right_side,
        noise_precision,
        degree.reshape(1, 256),
        var_precision,
        local_tiles,
        send_rows,
        halo_weights,
    )


def solution(mesh):
    placed = (
        P("dom", None),
        P("dom", None),
        P("dom"),
        P(),
        P(),
        P("dom", None, None, None),
        P("dom", None),
        P("dom"),
        P("dom", None),
        P("dom", None, None),
        P("dom", None),
        P("dom", None, None, None),
    )
    return jax.shard_map(
        local, mesh=mesh, in_specs=placed, out_specs=P("dom", None), check_vma=False
    )
```

time: 622 us -> 50.9 us (0.08)
  blocking collectives: 514 us -> 0 us
  Pallas kernels: 0 us -> 43.8 us
  starting transfers between devices: 37.8 us -> 0 us
  loops' own time: 18.8 us -> 0 us
  matrix products: 16.4 us -> 0 us
  between operations: 15.2 us -> 0.76 us
  local copies, waits for them, and re-layouts: 13.3 us -> 6.02 us
    psum x5 -> x0, blocking collectives: 514 us -> none  [the longest x3 301 us: squared_total(): return lax.psum(jnp.sum(vector * vector), 'dom')]
    pallas_call x0 -> x1, Pallas kernels: none -> 43.8 us  [local(): pl.pallas_call(kernel, out_shape=jax.ShapeDtypeStruct((256, 256), F32), i...]
    ppermute x12 -> x0, starting transfers between devices: 37.8 us -> none  [from_behind(): return lax.ppermute(block, axis, route)]
    another operation x6 -> x0, loops' own time: 18.8 us -> none  [local(): lax.fori_loop(0, tile_count[row_tile], accumulate_submatrix, start)]
    dot_general x21 -> x0, matrix products: 16.4 us -> none  [the longest x12 11.5 us: local(): jnp.einsum('ka,kv->av', border_weights[heading], arrived, precision=highe...]
  transfers between devices with their start and end apart: 12 -> 0, of which waited for: 0 -> 0; matrix products, arithmetic and copies ran while one was open for 3% -> 0% of each run, Pallas kernels for 0% -> 0%
where the time goes in v1:
time: 50.9 us; the launch traced here: 50.6 us
  Pallas kernels  43.8 us (86%)
  local copies, waits for them, and re-layouts  6.02 us (12%)
  between operations  0.76 us (1%)
    pallas_call x1, Pallas kernels, local(): pl.pallas_call(kernel, out_shape=jax.ShapeDtypeStruct((256, 256), F32), i...  43.8 us
    unnamed x23, local copies, waits for them, and re-layouts  6.02 us

profile of v1, /device:TPU:1, one launch (start us, length us, event | category | flops | bytes accessed | tf_op | source)
XLA Modules:
  0.0 50.6 jit_solution(4015145548634035215)
XLA Ops:
  0.0 0.0 copy-start.7
  0.0 0.0 copy-start.9
  0.0 0.0 copy-start.10
  0.7 0.0 copy-start.5
  0.7 0.0 copy-start.6
  0.7 0.0 copy-start.8
  0.7 0.0 copy-done.7
  0.7 0.0 copy-done.9
  0.8 0.0 copy-done.10
  0.8 0.6 %copy-done.5 = s32[1,4,64]{2,1,0:T(4,128)S(1)} copy-done((s32[1,4,64]{2,1,0:T(4,128)S(1)}, s32[1,4,64]{2,1,0:T(4,128)}, u32[]{:S(2)}) %copy-start.5) | copy-done | bytes 1048
  1.4 0.0 copy-done.6
  1.4 0.0 copy-done.8
  1.4 0.0 copy-start
  1.4 0.9 %copy-done = f32[256,256]{1,0:T(8,128)S(1)} copy-done((f32[256,256]{1,0:T(8,128)S(1)}, f32[256,256]{1,0:T(8,128)}, u32[]{:S(2)}) %copy-start) | copy-done | bytes 262168
  2.4 0.0 copy-start.1
  2.4 0.9 %copy-done.1 = f32[256,256]{1,0:T(8,128)S(1)} copy-done((f32[256,256]{1,0:T(8,128)S(1)}, f32[256,256]{1,0:T(8,128)}, u32[]{:S(2)}) %copy-start.1) | copy-done | bytes 262168
  3.3 0.0 copy-start.2
  3.3 0.9 %copy-done.2 = f32[2,2,128,128]{3,2,1,0:T(8,128)S(1)} copy-done((f32[2,2,128,128]{3,2,1,0:T(8,128)S(1)}, f32[2,2,128,128]{3,2,1,0:T(8,128)}, u32[]{:S(2)}) %copy-start.2) | copy-done | bytes 262168
  4.3 0.0 copy-start.3
  4.3 0.9 %copy-done.3 = bf16[256,256]{1,0:T(8,128)(2,1)S(1)} copy-done((bf16[256,256]{1,0:T(8,128)(2,1)S(1)}, bf16[256,256]{1,0:T(8,128)(2,1)}, u32[]{:S(2)}) %copy-start.3) | copy-done | bytes 131096
  5.2 0.0 copy-start.4
  5.2 0.9 %copy-done.4 = f32[1,4,64,128]{3,2,1,0:T(8,128)S(1)} copy-done((f32[1,4,64,128]{3,2,1,0:T(8,128)S(1)}, f32[1,4,64,128]{3,2,1,0:T(8,128)}, u32[]{:S(2)}) %copy-start.4) | copy-done | bytes 131096
  6.1 43.8 %conjugate_gradient.1 = f32[256,256]{1,0:T(8,128)S(1)} custom-call(f32[1]{0:T(128)} %bitcast.2.dependence_ref, s32[2,2]{1,0:T(2,128)S(1)} %copy-done.6, s32[2]{0:T(128)S(1)} %copy-done.8, s32[1,4]{1,0:T(1,128)S(1)} %copy-done.9, s32[1,4]{1,0:T(1,128)S(1)} %copy-done.10, f32[256,256]{1,0:T(8,128)S(1)} %copy-done, bf16[256,256]{1,0:T(8,128)(2,1)S(1)} %copy-done.3, ...), custom_call_target="tpu_custom_call" | custom-call | tf_op jit(solution)/shard_map/conjugate_gradient/pallas_call | solution.py:332
  49.9 0.7 %copy.15 = f32[256,256]{1,0:T(8,128)} copy(f32[256,256]{1,0:T(8,128)S(1)} %conjugate_gradient.1) | data formatting | bytes 524288
Async XLA Ops:
  0.0 0.7 %copy-start.7 = (f32[256]{0:T(256)S(1)}, f32[256]{0:T(256)}, u32[]{:S(2)}) copy-start(f32[256]{0:T(256)} %param.14) | copy-start | bytes 3076
  0.0 0.7 %copy-start.9 = (s32[1,4]{1,0:T(1,128)S(1)}, s32[1,4]{1,0:T(1,128)}, u32[]{:S(2)}) copy-start(s32[1,4]{1,0:T(1,128)} %halo_tile_ref.1) | copy-start | bytes 52
  0.0 0.7 %copy-start.10 = (s32[1,4]{1,0:T(1,128)S(1)}, s32[1,4]{1,0:T(1,128)}, u32[]{:S(2)}) copy-start(s32[1,4]{1,0:T(1,128)} %send_count_ref.1) | copy-start | bytes 52
  0.7 0.7 %copy-start.5 = (s32[1,4,64]{2,1,0:T(4,128)S(1)}, s32[1,4,64]{2,1,0:T(4,128)}, u32[]{:S(2)}) copy-start(s32[1,4,64]{2,1,0:T(4,128)} %rows_hbm.1) | copy-start | bytes 3076
  0.7 0.7 %copy-start.6 = (s32[2,2]{1,0:T(2,128)S(1)}, s32[2,2]{1,0:T(2,128)}, u32[]{:S(2)}) copy-start(s32[2,2]{1,0:T(2,128)} %tile_cols_ref.1) | copy-start | bytes 52
  0.7 0.7 %copy-start.8 = (s32[2]{0:T(128)S(1)}, s32[2]{0:T(128)}, u32[]{:S(2)}) copy-start(s32[2]{0:T(128)} %tile_count_ref.1) | copy-start | bytes 28
  1.4 1.0 %copy-start = (f32[256,256]{1,0:T(8,128)S(1)}, f32[256,256]{1,0:T(8,128)}, u32[]{:S(2)}) copy-start(f32[256,256]{1,0:T(8,128)} %right_hbm.1) | copy-start | bytes 786436
  2.4 0.9 %copy-start.1 = (f32[256,256]{1,0:T(8,128)S(1)}, f32[256,256]{1,0:T(8,128)}, u32[]{:S(2)}) copy-start(f32[256,256]{1,0:T(8,128)} %var_hbm.1) | copy-start | bytes 786436
  3.3 0.9 %copy-start.2 = (f32[2,2,128,128]{3,2,1,0:T(8,128)S(1)}, f32[2,2,128,128]{3,2,1,0:T(8,128)}, u32[]{:S(2)}) copy-start(f32[2,2,128,128]{3,2,1,0:T(8,128)} %tiles_hbm.1) | copy-start | bytes 786436
  4.3 0.9 %copy-start.3 = (bf16[256,256]{1,0:T(8,128)(2,1)S(1)}, bf16[256,256]{1,0:T(8,128)(2,1)}, u32[]{:S(2)}) copy-start(bf16[256,256]{1,0:T(8,128)(2,1)} %noise_hbm.1) | copy-start | bytes 393220
  5.2 0.9 %copy-start.4 = (f32[1,4,64,128]{3,2,1,0:T(8,128)S(1)}, f32[1,4,64,128]{3,2,1,0:T(8,128)}, u32[]{:S(2)}) copy-start(f32[1,4,64,128]{3,2,1,0:T(8,128)} %halo_hbm.1) | copy-start | bytes 393220

commit v2 on v1

v2 whole, which is shorter than its diff:
```python
import functools

import jax
import jax.numpy as jnp
from jax import lax
from jax.experimental import pallas as pl
from jax.experimental.pallas import tpu as pltpu
from jax.sharding import PartitionSpec as P

MESH = pl.DeviceIdType.MESH
GRID_W = 16
OFFSETS = (1, -1, GRID_W, -GRID_W)
REVERSE = (1, 0, 3, 2)
STAGES = ((1, 16), (16, 32))
F32 = jnp.float32
BF16 = jnp.bfloat16


def ring(distance, size):
    return min(distance, size - distance)


def farthest_first(stride, size):
    def hops(mask):
        if stride == 1:
            return max(ring(abs((a ^ mask) // 2 - a // 2), size // 2) for a in range(size))
        return max(
            ring(abs((a ^ mask) % 8 - a % 8), 8) + ring(abs((a ^ mask) // 8 - a // 8), size // 8)
            for a in range(size)
        )

    return sorted(range(1, size), key=lambda mask: -hops(mask))


def split(value):
    high = value.astype(BF16)
    low = (value - high.astype(F32)).astype(BF16)
    return high, low


def as_left(value):
    high, low = split(value)
    return jnp.concatenate([high, low, high], axis=1)


def as_right(value):
    high, low = split(value)
    return jnp.concatenate([high, low, high], axis=0)


def keep_left(ref, value):
    high, low = split(value)
    n = value.shape[1]
    ref[:, 0:n] = high
    ref[:, n : 2 * n] = high
    ref[:, 2 * n : 3 * n] = low


def keep_right(ref, value):
    high, low = split(value)
    n = value.shape[0]
    ref[0:n, :] = high
    ref[n : 2 * n, :] = high
    ref[2 * n : 3 * n, :] = low


def dot(a, b):
    return jnp.dot(a, b, preferred_element_type=F32)


def fold(value):
    rows, lanes = value.shape
    tile = jnp.sum(value.reshape(rows // 8, 8, lanes), axis=0)
    tile = tile[:, 0:128] + tile[:, 128:256]
    return jnp.sum(tile, axis=0, keepdims=True)


def total_of(row):
    return jnp.sum(row, axis=1, keepdims=True)


def kernel(
    right_hbm,
    noise_hbm,
    degree_hbm,
    dependence_ref,
    var_hbm,
    tiles_hbm,
    cols_hbm,
    count_hbm,
    border_hbm,
    rows_hbm,
    live_hbm,
    halo_hbm,
    out_ref,
    right_ref,
    noise_ref,
    degree_ref,
    var_ref,
    tiles_ref,
    cols_ref,
    count_ref,
    border_ref,
    rows_ref,
    live_ref,
    halo_ref,
    var_cat,
    local_cat,
    halo_cat,
    hop_cat,
    scatter,
    gather,
    basis,
    sent,
    received,
    sums_a,
    sums_b,
    load_sem,
    send_sem,
    recv_sem,
    sum_send_sem,
    sum_recv_sem,
):
    me = lax.axis_index("dom")
    pairs = {
        "right": (right_hbm, right_ref),
        "noise": (noise_hbm, noise_ref),
        "degree": (degree_hbm, degree_ref),
        "var": (var_hbm, var_ref),
        "tiles": (tiles_hbm, tiles_ref),
        "cols": (cols_hbm, cols_ref),
        "count": (count_hbm, count_ref),
        "border": (border_hbm, border_ref),
        "rows": (rows_hbm, rows_ref),
        "live": (live_hbm, live_ref),
        "halo": (halo_hbm, halo_ref),
    }
    loads = {
        name: pltpu.make_async_copy(src, dst, load_sem.at[i])
        for i, (name, (src, dst)) in enumerate(pairs.items())
    }
    for name in (
        "border",
        "halo",
        "right",
        "var",
        "live",
        "rows",
        "tiles",
        "cols",
        "count",
        "degree",
        "noise",
    ):
        loads[name].start()

    column = jnp.bitwise_and(me, GRID_W - 1)
    line = jnp.right_shift(me, 4)
    usable = (column < GRID_W - 1, column > 0, line < 512 // GRID_W - 1, line > 0)

    odd = jnp.bitwise_and(me, 1)

    def partners(stride, size):
        return [(j, jnp.bitwise_xor(me, j * stride)) for j in farthest_first(stride, size)]

    barrier = pltpu.get_barrier_semaphore()
    for c in range(4):

        @pl.when(usable[c])
        def _():
            pl.semaphore_signal(barrier, inc=1, device_id=(me + OFFSETS[c],), device_id_type=MESH)

    greeted = 0
    for stride, size in STAGES:
        for _, partner in partners(stride, size):
            pl.semaphore_signal(barrier, inc=1, device_id=(partner,), device_id_type=MESH)
            greeted += 1

    for c in range(4):

        @pl.when(jnp.logical_not(usable[c]))
        def _():
            for k in range(2):
                received[k, 64 * c : 64 * c + 64, :] = jnp.zeros((64, 256), F32)

    loads["border"].wait()
    loads["halo"].wait()
    for c in range(4):
        tile = border_ref[0, c]
        weights = halo_ref[0, c]
        block = jnp.concatenate(
            [jnp.where(tile == r, weights, jnp.zeros_like(weights)) for r in range(2)], axis=1
        )
        keep_left(halo_cat.at[64 * c : 64 * c + 64, :], block)
    loads["right"].wait()
    field = right_ref[...]
    field_cat = as_right(field)
    outgoing = dot(halo_cat[...], field_cat)

    pl.semaphore_wait(barrier, greeted + sum(u.astype(jnp.int32) for u in usable))

    def copy(k, c, to):
        return pltpu.make_async_remote_copy(
            src_ref=sent.at[k, 64 * c : 64 * c + 64, :],
            dst_ref=received.at[k, 64 * to : 64 * to + 64, :],
            send_sem=send_sem.at[k, c],
            recv_sem=recv_sem.at[k, to],
            device_id=(me + OFFSETS[c],),
            device_id_type=MESH,
        )

    def start(k):
        for c in (2, 3, 0, 1):
            pl.when(usable[c])(copy(k, c, REVERSE[c]).start)

    def finish(k):
        for c in (0, 1, 3, 2):
            pl.when(usable[c])(copy(k, c, c).wait_recv)

    def last(i, device):
        return pltpu.make_async_remote_copy(
            src_ref=sent.at[2, 64 * i : 64 * i + 64, :],
            dst_ref=received.at[2, 64 * i : 64 * i + 64, :],
            send_sem=send_sem.at[2, i],
            recv_sem=recv_sem.at[2, i],
            device_id=(device,),
            device_id_type=MESH,
        )

    across = GRID_W * (2 * odd - 1)
    down, up = usable[3], usable[2]
    even = odd == 0
    crosses = jnp.logical_or(jnp.logical_and(even, down), jnp.logical_and(odd == 1, up))
    crossed = jnp.logical_or(jnp.logical_and(even, up), jnp.logical_and(odd == 1, down))
    from_slots = pl.ds(pl.multiple_of(192 - 64 * odd, 64), 64)
    to_slots = pl.ds(pl.multiple_of(128 + 64 * odd, 64), 64)

    @pl.when(jnp.logical_not(usable[0]))
    def _():
        received[2, 0:64, :] = jnp.zeros((64, 256), F32)

    @pl.when(jnp.logical_not(crossed))
    def _():
        received[2, 64:128, :] = jnp.zeros((64, 256), F32)

    sent[0] = outgoing
    start(0)

    loads["var"].wait()
    keep_right(var_cat, var_ref[...])

    loads["live"].wait()
    loads["rows"].wait()
    places = []
    slot = lax.broadcasted_iota(jnp.int32, (1, 64), 1)
    for c in range(4):
        place = rows_ref[0, c : c + 1, :] + border_ref[0, c] * 128
        places.append(jnp.where(slot < live_ref[0, c], place, -1))
    places = jnp.concatenate(places, axis=1)
    hot = lax.broadcasted_iota(jnp.int32, (256, 256), 0) == places
    hot_wide = jnp.where(hot, 1.0, 0.0)
    hot = hot_wide.astype(BF16)
    scatter[:, 0:256] = hot
    scatter[:, 256:512] = hot

    for name in ("tiles", "cols", "count", "degree"):
        loads[name].wait()
    dependence = dependence_ref[0]
    on_diagonal = lax.broadcasted_iota(jnp.int32, (256, 256), 0) == lax.broadcasted_iota(
        jnp.int32, (256, 256), 1
    )
    diagonal = jnp.where(on_diagonal, degree_ref[...], 0.0)
    for r in range(2):
        row = []
        for s in range(2):
            block = jnp.zeros((128, 128), F32)
            for j in range(2):
                used = jnp.logical_and(cols_ref[r, j] == s, count_ref[r] > j)
                block = jnp.where(used, tiles_ref[r, j], block)
            row.append(block)
        block_row = diagonal[128 * r : 128 * r + 128] - dependence * jnp.concatenate(row, axis=1)
        keep_left(local_cat.at[128 * r : 128 * r + 128, :], block_row)
    loads["noise"].wait()
    noise = noise_ref[...].astype(F32)

    hop_cat[:, 0:256] = dot(halo_cat[:, 0:256], hot).astype(BF16)
    hop_cat[:, 256:512] = hop_cat[:, 0:256]
    hop_cat[:, 512:768] = dot(halo_cat[:, 512:768], hot).astype(BF16)
    gather[...] = hot_wide.T.astype(BF16)

    basis[0] = field
    moments = [fold(field * field)]
    for k in range(2):
        near = dot(as_left(dot(local_cat[...], field_cat)), var_cat[...]) + noise * field
        next_near = dot(halo_cat[...], as_right(near))
        finish(k)
        arrived = dot(as_left(received[k]), var_cat[...])
        arrived_cat = as_right(arrived)
        if k == 0:
            sent[1] = next_near - dependence * dot(hop_cat[...], arrived_cat)
            start(1)
        else:
            hop = jnp.concatenate([hop_cat[64:128, :], hop_cat[from_slots, :]], axis=0)
            crossing = jnp.where(even, next_near[192:256], next_near[128:192])
            outgoing = jnp.concatenate([next_near[64:128], crossing], axis=0)
            sent[2, 0:128, :] = outgoing - dependence * dot(hop, arrived_cat)
            pl.when(crosses)(last(1, me + across).start)
            pl.when(usable[1])(last(0, me - 1).start)
        image = near - dependence * dot(scatter[...], arrived_cat[0:512])
        moments.append(fold(field * image))
        moments.append(fold(image * image))
        field = image
        field_cat = as_right(field)
        basis[k + 1] = field

    mapped = dot(as_left(field), var_cat[...])
    near = fold(dot(local_cat[...], field_cat) * mapped + noise * (field * field))
    high, low = split(mapped)
    picks = jnp.concatenate([gather[0:64, :], gather[to_slots, :]], axis=0)
    picked = dot(picks, high) + dot(picks, low)
    picked = (-2.0 * dependence) * picked
    lane = lax.broadcasted_iota(jnp.int32, (8, 128), 1)
    line_of = lax.broadcasted_iota(jnp.int32, (8, 128), 0)

    def pack(rows):
        tile = jnp.concatenate(rows, axis=0)
        for shift in (64, 32, 16):
            tile = tile + pltpu.roll(tile, shift, 1)
        return jnp.sum(jnp.where(lane // 16 == line_of, tile, 0.0), axis=0, keepdims=True)

    early = pack(moments + [near, jnp.zeros((2, 128), F32)])
    pl.when(usable[0])(last(0, me + 1).wait_recv)
    pl.when(crossed)(last(1, me - across).wait_recv)
    cross = fold(picked * received[2, 0:128, :])
    for shift in (64, 32, 16):
        cross = cross + pltpu.roll(cross, shift, 1)
    total = early + jnp.where(lane[0:1] // 16 == 5, cross, 0.0)

    pending = []
    for n, ((stride, size), sums) in enumerate(zip(STAGES, (sums_a, sums_b))):
        sums[0:1, :] = total
        for j, partner in partners(stride, size):
            pltpu.make_async_remote_copy(
                src_ref=sums.at[0:1, :],
                dst_ref=sums.at[j : j + 1, :],
                send_sem=sum_send_sem.at[n],
                recv_sem=sum_recv_sem.at[n],
                device_id=(partner,),
                device_id_type=MESH,
            ).start()
        whole = pltpu.make_async_remote_copy(
            src_ref=sums.at[1:size, :],
            dst_ref=sums.at[1:size, :],
            send_sem=sum_send_sem.at[n],
            recv_sem=sum_recv_sem.at[n],
            device_id=(me,),
            device_id_type=MESH,
        )
        whole.wait_recv()
        total = jnp.sum(sums[...], axis=0, keepdims=True)
        pending.append(whole)

    m = [
        jnp.where(lane[0:1] < 16, total if k == 0 else pltpu.roll(total, 128 - 16 * k, 1), 0.0)
        for k in range(6)
    ]
    rr0 = total_of(m[0])
    a0 = rr0 / total_of(m[1])
    rr1 = total_of(m[0] - 2.0 * a0 * m[1] + a0 * a0 * m[2])
    g0 = 1.0 + rr1 / rr0
    g1 = -a0
    a1 = rr1 / total_of(g0 * g0 * m[1] + 2.0 * g0 * g1 * m[2] + g1 * g1 * m[3])
    e1 = -a0 - a1 * g0
    e2 = -a1 * g1
    rr2 = total_of(
        m[0] + 2.0 * e1 * m[1] + (e1 * e1 + 2.0 * e2) * m[2] + 2.0 * e1 * e2 * m[3] + e2 * e2 * m[4]
    )
    b1 = rr2 / rr1
    f0 = 1.0 + b1 * g0
    f1 = e1 + b1 * g1
    f2 = e2
    a2 = rr2 / total_of(
        f0 * f0 * m[1]
        + 2.0 * f0 * f1 * m[2]
        + (f1 * f1 + 2.0 * f0 * f2) * m[3]
        + 2.0 * f1 * f2 * m[4]
        + f2 * f2 * m[5]
    )
    c0 = a0 + a1 * g0 + a2 * f0
    c1 = a1 * g1 + a2 * f1
    c2 = a2 * f2
    out_ref[...] = c0 * basis[0] + c1 * basis[1] + c2 * basis[2]

    for whole in pending:
        whole.wait_send()
    for k in range(2):
        for c in range(4):
            pl.when(usable[c])(copy(k, c, REVERSE[c]).wait_send)
    pl.when(usable[1])(last(0, me - 1).wait_send)
    pl.when(crosses)(last(1, me + across).wait_send)


def local(
    right_side,
    noise_precision,
    degree,
    dependence,
    var_precision,
    local_tiles,
    tile_cols,
    tile_count,
    halo_tile,
    send_rows,
    send_count,
    halo_weights,
):
    operands = (
        right_side,
        noise_precision,
        degree.reshape(1, 256),
        dependence.reshape(1),
        var_precision,
        local_tiles,
        tile_cols,
        tile_count,
        halo_tile,
        send_rows,
        send_count,
        halo_weights,
    )
    operands = [
        x if x.size == 1 else pltpu.with_memory_space_constraint(x, pltpu.HBM) for x in operands
    ]
    specs = [pl.BlockSpec(memory_space=pltpu.SMEM if x.size == 1 else pltpu.HBM) for x in operands]
    held = (
        pltpu.VMEM((256, 256), F32),
        pltpu.VMEM((256, 256), BF16),
        pltpu.VMEM((1, 256), F32),
        pltpu.VMEM((256, 256), F32),
        pltpu.VMEM((2, 2, 128, 128), F32),
        pltpu.SMEM((2, 2), jnp.int32),
        pltpu.SMEM((2,), jnp.int32),
        pltpu.SMEM((1, 4), jnp.int32),
        pltpu.VMEM((1, 4, 64), jnp.int32),
        pltpu.SMEM((1, 4), jnp.int32),
        pltpu.VMEM((1, 4, 64, 128), F32),
    )
    return pl.pallas_call(
        kernel,
        out_shape=pltpu.VMEM((256, 256), F32),
        in_specs=specs,
        out_specs=pl.BlockSpec(memory_space=pltpu.VMEM),
        scratch_shapes=list(held)
        + [
            pltpu.VMEM((768, 256), BF16),
            pltpu.VMEM((256, 768), BF16),
            pltpu.VMEM((256, 768), BF16),
            pltpu.VMEM((256, 768), BF16),
            pltpu.VMEM((256, 512), BF16),
            pltpu.VMEM((256, 256), BF16),
            pltpu.VMEM((3, 256, 256), F32),
            pltpu.VMEM((3, 256, 256), F32),
            pltpu.VMEM((3, 256, 256), F32),
            pltpu.VMEM((STAGES[0][1], 128), F32),
            pltpu.VMEM((STAGES[1][1], 128), F32),
            pltpu.SemaphoreType.DMA((11,)),
            pltpu.SemaphoreType.DMA((3, 4)),
            pltpu.SemaphoreType.DMA((3, 4)),
            pltpu.SemaphoreType.DMA((2,)),
            pltpu.SemaphoreType.DMA((2,)),
        ],
        compiler_params=pltpu.CompilerParams(
            collective_id=0, has_side_effects=True, vmem_limit_bytes=48 * 1024 * 1024
        ),
        name="conjugate_gradient",
    )(*operands)


def solution(mesh):
    placed = (
        P("dom", None),
        P("dom", None),
        P("dom"),
        P(),
        P(),
        P("dom", None, None, None),
        P("dom", None),
        P("dom"),
        P("dom", None),
        P("dom", None, None),
        P("dom", None),
        P("dom", None, None, None),
    )
    return jax.shard_map(
        local, mesh=mesh, in_specs=placed, out_specs=P("dom", None), check_vma=False
    )
```

time: 50.9 us -> 40.7 us (0.80)
  local copies, waits for them, and re-layouts: 6.02 us -> 0.71 us
  Pallas kernels: 43.8 us -> 39.2 us
    unnamed x23 -> x1, local copies, waits for them, and re-layouts: 6.02 us -> 0.71 us
    pallas_call x1, Pallas kernels: 43.8 us -> 39.2 us  [local(): pl.pallas_call(kernel, out_shape=pltpu.VMEM((256, 256), F32), in_specs=sp...]
where the time goes in v2:
time: 40.7 us; the launch traced here: 40.6 us
  Pallas kernels  39.2 us (96%)
  local copies, waits for them, and re-layouts  0.71 us (2%)
  between operations  0.66 us (2%)
    pallas_call x1, Pallas kernels, local(): pl.pallas_call(kernel, out_shape=pltpu.VMEM((256, 256), F32), in_specs=sp...  39.2 us

profile of v2, /device:TPU:1, one launch (start us, length us, event | category | flops | bytes accessed | tf_op | source)
XLA Modules:
  0.0 40.6 jit_solution(995352931900186548)
XLA Ops:
  0.7 39.2 %conjugate_gradient.1 = f32[256,256]{1,0:T(8,128)S(1)} custom-call(f32[256,256]{1,0:T(8,128)} %right_hbm.1, bf16[256,256]{1,0:T(8,128)(2,1)} %noise_hbm.1, f32[1,256]{1,0:T(1,128)} %bitcast.3, f32[1]{0:T(128)} %bitcast.2.dependence_ref, f32[256,256]{1,0:T(8,128)} %var_hbm.1, f32[2,2,128,128]{3,2,1,0:T(8,128)} %tiles_hbm.1, s32[2,2]{1,0:T(2,128)} %cols_hbm.1, ...), custom_call_target="tpu_custom_call" | custom-call | tf_op jit(solution)/shard_map/conjugate_gradient/pallas_call | solution.py:448
  39.9 0.7 %copy.14 = f32[256,256]{1,0:T(8,128)} copy(f32[256,256]{1,0:T(8,128)S(1)} %conjugate_gradient.1) | data formatting | bytes 524288

commit v3 on v2

--- a/solution.py
+++ b/solution.py
@@ -139,19 +139,7 @@
         name: pltpu.make_async_copy(src, dst, load_sem.at[i])
         for i, (name, (src, dst)) in enumerate(pairs.items())
     }
-    for name in (
-        "border",
-        "halo",
-        "right",
-        "var",
-        "live",
-        "rows",
-        "tiles",
-        "cols",
-        "count",
-        "degree",
-        "noise",
-    ):
+    for name in ("border", "halo", "right"):
         loads[name].start()
 
     column = jnp.bitwise_and(me, GRID_W - 1)
@@ -175,6 +163,9 @@
         for _, partner in partners(stride, size):
             pl.semaphore_signal(barrier, inc=1, device_id=(partner,), device_id_type=MESH)
             greeted += 1
+
+    for name in ("var", "live", "rows", "tiles", "cols", "count", "degree", "noise"):
+        loads[name].start()
 
     for c in range(4):
 
@@ -209,15 +200,18 @@
             device_id_type=MESH,
         )
 
-    def start(k):
-        for c in (2, 3, 0, 1):
+    groups = ((0, 1), (2, 3))
+
+    def start(k, group):
+        for c in groups[group]:
             pl.when(usable[c])(copy(k, c, REVERSE[c]).start)
 
-    def finish(k):
-        for c in (0, 1, 3, 2):
+    def finish(k, group):
+        for c in groups[group]:
             pl.when(usable[c])(copy(k, c, c).wait_recv)
 
     def last(i, device):
+        i = 1 - i
         return pltpu.make_async_remote_copy(
             src_ref=sent.at[2, 64 * i : 64 * i + 64, :],
             dst_ref=received.at[2, 64 * i : 64 * i + 64, :],
@@ -237,14 +231,15 @@
 
     @pl.when(jnp.logical_not(usable[0]))
     def _():
-        received[2, 0:64, :] = jnp.zeros((64, 256), F32)
+        received[2, 64:128, :] = jnp.zeros((64, 256), F32)
 
     @pl.when(jnp.logical_not(crossed))
     def _():
-        received[2, 64:128, :] = jnp.zeros((64, 256), F32)
+        received[2, 0:64, :] = jnp.zeros((64, 256), F32)
 
     sent[0] = outgoing
-    start(0)
+    start(0, 1)
+    start(0, 0)
 
     loads["var"].wait()
     keep_right(var_cat, var_ref[...])
@@ -260,8 +255,9 @@
     hot = lax.broadcasted_iota(jnp.int32, (256, 256), 0) == places
     hot_wide = jnp.where(hot, 1.0, 0.0)
     hot = hot_wide.astype(BF16)
-    scatter[:, 0:256] = hot
-    scatter[:, 256:512] = hot
+    for group in range(2):
+        scatter[group, :, 0:128] = hot[:, 128 * group : 128 * group + 128]
+        scatter[group, :, 128:256] = hot[:, 128 * group : 128 * group + 128]
 
     for name in ("tiles", "cols", "count", "degree"):
         loads[name].wait()
@@ -283,9 +279,13 @@
     loads["noise"].wait()
     noise = noise_ref[...].astype(F32)
 
-    hop_cat[:, 0:256] = dot(halo_cat[:, 0:256], hot).astype(BF16)
-    hop_cat[:, 256:512] = hop_cat[:, 0:256]
-    hop_cat[:, 512:768] = dot(halo_cat[:, 512:768], hot).astype(BF16)
+    hop_high = dot(halo_cat[:, 0:256], hot).astype(BF16)
+    hop_low = dot(halo_cat[:, 512:768], hot).astype(BF16)
+    for group in range(2):
+        part = slice(128 * group, 128 * group + 128)
+        hop_cat[group, :, 0:128] = hop_high[:, part]
+        hop_cat[group, :, 128:256] = hop_high[:, part]
+        hop_cat[group, :, 256:384] = hop_low[:, part]
     gather[...] = hot_wide.T.astype(BF16)
 
     basis[0] = field
@@ -293,20 +293,29 @@
     for k in range(2):
         near = dot(as_left(dot(local_cat[...], field_cat)), var_cat[...]) + noise * field
         next_near = dot(halo_cat[...], as_right(near))
-        finish(k)
-        arrived = dot(as_left(received[k]), var_cat[...])
-        arrived_cat = as_right(arrived)
+        finish(k, 0)
+        first = as_right(dot(as_left(received[k, 0:128, :]), var_cat[...]))
+        image = near - dependence * dot(scatter[0], first[0:256])
         if k == 0:
-            sent[1] = next_near - dependence * dot(hop_cat[...], arrived_cat)
-            start(1)
+            ready = next_near - dependence * dot(hop_cat[0], first)
         else:
-            hop = jnp.concatenate([hop_cat[64:128, :], hop_cat[from_slots, :]], axis=0)
+            rows = jnp.concatenate([hop_cat[0, from_slots, :], hop_cat[0, 64:128, :]], axis=0)
             crossing = jnp.where(even, next_near[192:256], next_near[128:192])
-            outgoing = jnp.concatenate([next_near[64:128], crossing], axis=0)
-            sent[2, 0:128, :] = outgoing - dependence * dot(hop, arrived_cat)
+            ready = jnp.concatenate([crossing, next_near[64:128]], axis=0)
+            ready = ready - dependence * dot(rows, first)
+        finish(k, 1)
+        second = as_right(dot(as_left(received[k, 128:256, :]), var_cat[...]))
+        if k == 0:
+            for group in (1, 0):
+                part = slice(128 * group, 128 * group + 128)
+                sent[1, part, :] = ready[part] - dependence * dot(hop_cat[1, part, :], second)
+                start(1, group)
+        else:
+            rows = jnp.concatenate([hop_cat[1, from_slots, :], hop_cat[1, 64:128, :]], axis=0)
+            sent[2, 0:128, :] = ready - dependence * dot(rows, second)
             pl.when(crosses)(last(1, me + across).start)
             pl.when(usable[1])(last(0, me - 1).start)
-        image = near - dependence * dot(scatter[...], arrived_cat[0:512])
+        image = image - dependence * dot(scatter[1], second[0:256])
         moments.append(fold(field * image))
         moments.append(fold(image * image))
         field = image
@@ -316,25 +325,21 @@
     mapped = dot(as_left(field), var_cat[...])
     near = fold(dot(local_cat[...], field_cat) * mapped + noise * (field * field))
     high, low = split(mapped)
-    picks = jnp.concatenate([gather[0:64, :], gather[to_slots, :]], axis=0)
+    picks = jnp.concatenate([gather[to_slots, :], gather[0:64, :]], axis=0)
     picked = dot(picks, high) + dot(picks, low)
     picked = (-2.0 * dependence) * picked
     lane = lax.broadcasted_iota(jnp.int32, (8, 128), 1)
     line_of = lax.broadcasted_iota(jnp.int32, (8, 128), 0)
 
     def pack(rows):
-        tile = jnp.concatenate(rows, axis=0)
-        for shift in (64, 32, 16):
-            tile = tile + pltpu.roll(tile, shift, 1)
-        return jnp.sum(jnp.where(lane // 16 == line_of, tile, 0.0), axis=0, keepdims=True)
+        tile = jnp.sum(jnp.concatenate(rows, axis=0), axis=1, keepdims=True)
+        return jnp.sum(jnp.where(lane == line_of, tile, 0.0), axis=0, keepdims=True)
 
     early = pack(moments + [near, jnp.zeros((2, 128), F32)])
     pl.when(usable[0])(last(0, me + 1).wait_recv)
     pl.when(crossed)(last(1, me - across).wait_recv)
     cross = fold(picked * received[2, 0:128, :])
-    for shift in (64, 32, 16):
-        cross = cross + pltpu.roll(cross, shift, 1)
-    total = early + jnp.where(lane[0:1] // 16 == 5, cross, 0.0)
+    total = early + jnp.where(lane[0:1] == 5, total_of(cross), 0.0)
 
     pending = []
     for n, ((stride, size), sums) in enumerate(zip(STAGES, (sums_a, sums_b))):
@@ -360,26 +365,22 @@
         total = jnp.sum(sums[...], axis=0, keepdims=True)
         pending.append(whole)
 
-    m = [
-        jnp.where(lane[0:1] < 16, total if k == 0 else pltpu.roll(total, 128 - 16 * k, 1), 0.0)
-        for k in range(6)
-    ]
-    rr0 = total_of(m[0])
-    a0 = rr0 / total_of(m[1])
-    rr1 = total_of(m[0] - 2.0 * a0 * m[1] + a0 * a0 * m[2])
-    g0 = 1.0 + rr1 / rr0
+    m = [total[:, k : k + 1] for k in range(6)]
+    a0 = m[0] / m[1]
+    rr1 = m[0] - 2.0 * a0 * m[1] + a0 * a0 * m[2]
+    g0 = 1.0 + rr1 / m[0]
     g1 = -a0
-    a1 = rr1 / total_of(g0 * g0 * m[1] + 2.0 * g0 * g1 * m[2] + g1 * g1 * m[3])
+    a1 = rr1 / (g0 * g0 * m[1] + 2.0 * g0 * g1 * m[2] + g1 * g1 * m[3])
     e1 = -a0 - a1 * g0
     e2 = -a1 * g1
-    rr2 = total_of(
+    rr2 = (
         m[0] + 2.0 * e1 * m[1] + (e1 * e1 + 2.0 * e2) * m[2] + 2.0 * e1 * e2 * m[3] + e2 * e2 * m[4]
     )
     b1 = rr2 / rr1
     f0 = 1.0 + b1 * g0
     f1 = e1 + b1 * g1
     f2 = e2
-    a2 = rr2 / total_of(
+    a2 = rr2 / (
         f0 * f0 * m[1]
         + 2.0 * f0 * f1 * m[2]
         + (f1 * f1 + 2.0 * f0 * f2) * m[3]
@@ -455,8 +456,8 @@
             pltpu.VMEM((768, 256), BF16),
             pltpu.VMEM((256, 768), BF16),
             pltpu.VMEM((256, 768), BF16),
-            pltpu.VMEM((256, 768), BF16),
-            pltpu.VMEM((256, 512), BF16),
+            pltpu.VMEM((2, 256, 384), BF16),
+            pltpu.VMEM((2, 256, 256), BF16),
             pltpu.VMEM((256, 256), BF16),
             pltpu.VMEM((3, 256, 256), F32),
             pltpu.VMEM((3, 256, 256), F32),

time: 40.7 us -> 39.9 us (0.980)
  Pallas kernels: 39.2 us -> 38.4 us
    pallas_call x1, Pallas kernels: 39.2 us -> 38.4 us  [local(): pl.pallas_call(kernel, out_shape=pltpu.VMEM((256, 256), F32), in_specs=sp...]
where the time goes in v3:
time: 39.9 us; the launch traced here: 39.8 us
  Pallas kernels  38.4 us (96%)
  local copies, waits for them, and re-layouts  0.71 us (2%)
  between operations  0.66 us (2%)
    pallas_call x1, Pallas kernels, local(): pl.pallas_call(kernel, out_shape=pltpu.VMEM((256, 256), F32), in_specs=sp...  38.4 us

profile of v3, /device:TPU:1, one launch (start us, length us, event | category | flops | bytes accessed | tf_op | source)
XLA Modules:
  0.0 39.8 jit_solution(17952585183510380227)
XLA Ops:
  0.7 38.4 %conjugate_gradient.1 = f32[256,256]{1,0:T(8,128)S(1)} custom-call(f32[256,256]{1,0:T(8,128)} %right_hbm.1, bf16[256,256]{1,0:T(8,128)(2,1)} %noise_hbm.1, f32[1,256]{1,0:T(1,128)} %bitcast.3, f32[1]{0:T(128)} %bitcast.2.dependence_ref, f32[256,256]{1,0:T(8,128)} %var_hbm.1, f32[2,2,128,128]{3,2,1,0:T(8,128)} %tiles_hbm.1, s32[2,2]{1,0:T(2,128)} %cols_hbm.1, ...), custom_call_target="tpu_custom_call" | custom-call | tf_op jit(solution)/shard_map/conjugate_gradient/pallas_call | solution.py:449
  39.1 0.7 %copy.14 = f32[256,256]{1,0:T(8,128)} copy(f32[256,256]{1,0:T(8,128)S(1)} %conjugate_gradient.1) | data formatting | bytes 524288

commit v4 on v3

--- a/solution.py
+++ b/solution.py
@@ -14,6 +14,18 @@
 STAGES = ((1, 16), (16, 32))
 F32 = jnp.float32
 BF16 = jnp.bfloat16
+
+
+def partners_by_bit():
+    groups = {}
+    for mask in range(1, 16):
+        groups.setdefault(1 << (mask.bit_length() - 1), []).append(mask)
+    for z in range(8):
+        for x in range(4):
+            if z or x:
+                bit = 16 << (z.bit_length() - 1) if z else 128 << (x.bit_length() - 1)
+                groups.setdefault(bit, []).append(16 * z + 128 * x)
+    return groups
 
 
 def ring(distance, size):
@@ -120,6 +132,7 @@
     recv_sem,
     sum_send_sem,
     sum_recv_sem,
+    answer_sem,
 ):
     me = lax.axis_index("dom")
     pairs = {
@@ -158,11 +171,15 @@
         def _():
             pl.semaphore_signal(barrier, inc=1, device_id=(me + OFFSETS[c],), device_id_type=MESH)
 
-    greeted = 0
-    for stride, size in STAGES:
-        for _, partner in partners(stride, size):
-            pl.semaphore_signal(barrier, inc=1, device_id=(partner,), device_id_type=MESH)
-            greeted += 1
+    for bit, masks in partners_by_bit().items():
+
+        @pl.when(jnp.bitwise_and(me, bit) == 0)
+        def _():
+            for mask in masks:
+                greet = jnp.bitwise_xor(me, mask)
+                pl.semaphore_signal(barrier, inc=1, device_id=(greet,), device_id_type=MESH)
+
+    earlier = column + 4 * jnp.bitwise_and(line, 7) + jnp.right_shift(me, 7)
 
     for name in ("var", "live", "rows", "tiles", "cols", "count", "degree", "noise"):
         loads[name].start()
@@ -188,7 +205,7 @@
     field_cat = as_right(field)
     outgoing = dot(halo_cat[...], field_cat)
 
-    pl.semaphore_wait(barrier, greeted + sum(u.astype(jnp.int32) for u in usable))
+    pl.semaphore_wait(barrier, earlier + sum(u.astype(jnp.int32) for u in usable))
 
     def copy(k, c, to):
         return pltpu.make_async_remote_copy(
@@ -240,6 +257,15 @@
     sent[0] = outgoing
     start(0, 1)
     start(0, 0)
+
+    for bit, masks in partners_by_bit().items():
+
+        @pl.when(jnp.bitwise_and(me, bit) != 0)
+        def _():
+            for mask in masks:
+                answer = jnp.bitwise_xor(me, mask)
+                pl.semaphore_signal(answer_sem, inc=1, device_id=(answer,), device_id_type=MESH)
+
 
     loads["var"].wait()
     keep_right(var_cat, var_ref[...])
@@ -339,6 +365,12 @@
     pl.when(usable[0])(last(0, me + 1).wait_recv)
     pl.when(crossed)(last(1, me - across).wait_recv)
     cross = fold(picked * received[2, 0:128, :])
+    later = sum(size - 1 for _, size in STAGES) - earlier
+
+    @pl.when(later > 0)
+    def _():
+        pl.semaphore_wait(answer_sem, later)
+
     total = early + jnp.where(lane[0:1] == 5, total_of(cross), 0.0)
 
     pending = []
@@ -469,6 +501,7 @@
             pltpu.SemaphoreType.DMA((3, 4)),
             pltpu.SemaphoreType.DMA((2,)),
             pltpu.SemaphoreType.DMA((2,)),
+            pltpu.SemaphoreType.REGULAR,
         ],
         compiler_params=pltpu.CompilerParams(
             collective_id=0, has_side_effects=True, vmem_limit_bytes=48 * 1024 * 1024

time: 39.9 us -> 39.2 us (0.982)
  Pallas kernels: 38.4 us -> 37.7 us
    pallas_call x1, Pallas kernels: 38.4 us -> 37.7 us  [local(): pl.pallas_call(kernel, out_shape=pltpu.VMEM((256, 256), F32), in_specs=sp...]
where the time goes in v4:
time: 39.2 us; the launch traced here: 39 us
  Pallas kernels  37.7 us (96%)
  local copies, waits for them, and re-layouts  0.71 us (2%)
  between operations  0.66 us (2%)
    pallas_call x1, Pallas kernels, local(): pl.pallas_call(kernel, out_shape=pltpu.VMEM((256, 256), F32), in_specs=sp...  37.7 us

profile of v4, /device:TPU:1, one launch (start us, length us, event | category | flops | bytes accessed | tf_op | source)
XLA Modules:
  0.0 39.0 jit_solution(8145645090321293285)
XLA Ops:
  0.7 37.7 %conjugate_gradient.1 = f32[256,256]{1,0:T(8,128)S(1)} custom-call(f32[256,256]{1,0:T(8,128)} %right_hbm.1, bf16[256,256]{1,0:T(8,128)(2,1)} %noise_hbm.1, f32[1,256]{1,0:T(1,128)} %bitcast.3, f32[1]{0:T(128)} %bitcast.2.dependence_ref, f32[256,256]{1,0:T(8,128)} %var_hbm.1, f32[2,2,128,128]{3,2,1,0:T(8,128)} %tiles_hbm.1, s32[2,2]{1,0:T(2,128)} %cols_hbm.1, ...), custom_call_target="tpu_custom_call" | custom-call | tf_op jit(solution)/shard_map/conjugate_gradient/pallas_call | solution.py:481
  38.3 0.7 %copy.14 = f32[256,256]{1,0:T(8,128)} copy(f32[256,256]{1,0:T(8,128)S(1)} %conjugate_gradient.1) | data formatting | bytes 524288

commit v5 on v4

--- a/solution.py
+++ b/solution.py
@@ -136,7 +136,8 @@
 ):
     me = lax.axis_index("dom")
     pairs = {
-        "right": (right_hbm, right_ref),
+        "right": (right_hbm.at[0:128, :], right_ref.at[0:128, :]),
+        "right_too": (right_hbm.at[128:256, :], right_ref.at[128:256, :]),
         "noise": (noise_hbm, noise_ref),
         "degree": (degree_hbm, degree_ref),
         "var": (var_hbm, var_ref),
@@ -152,7 +153,7 @@
         name: pltpu.make_async_copy(src, dst, load_sem.at[i])
         for i, (name, (src, dst)) in enumerate(pairs.items())
     }
-    for name in ("border", "halo", "right"):
+    for name in ("right", "right_too", "halo", "border"):
         loads[name].start()
 
     column = jnp.bitwise_and(me, GRID_W - 1)
@@ -190,22 +191,6 @@
         def _():
             for k in range(2):
                 received[k, 64 * c : 64 * c + 64, :] = jnp.zeros((64, 256), F32)
-
-    loads["border"].wait()
-    loads["halo"].wait()
-    for c in range(4):
-        tile = border_ref[0, c]
-        weights = halo_ref[0, c]
-        block = jnp.concatenate(
-            [jnp.where(tile == r, weights, jnp.zeros_like(weights)) for r in range(2)], axis=1
-        )
-        keep_left(halo_cat.at[64 * c : 64 * c + 64, :], block)
-    loads["right"].wait()
-    field = right_ref[...]
-    field_cat = as_right(field)
-    outgoing = dot(halo_cat[...], field_cat)
-
-    pl.semaphore_wait(barrier, earlier + sum(u.astype(jnp.int32) for u in usable))
 
     def copy(k, c, to):
         return pltpu.make_async_remote_copy(
@@ -238,15 +223,15 @@
             device_id_type=MESH,
         )
 
-    across = GRID_W * (2 * odd - 1)
+    across = GRID_W * (1 - 2 * odd)
     down, up = usable[3], usable[2]
     even = odd == 0
-    crosses = jnp.logical_or(jnp.logical_and(even, down), jnp.logical_and(odd == 1, up))
-    crossed = jnp.logical_or(jnp.logical_and(even, up), jnp.logical_and(odd == 1, down))
-    from_slots = pl.ds(pl.multiple_of(192 - 64 * odd, 64), 64)
-    to_slots = pl.ds(pl.multiple_of(128 + 64 * odd, 64), 64)
-
-    @pl.when(jnp.logical_not(usable[0]))
+    crosses = jnp.logical_or(jnp.logical_and(even, up), jnp.logical_and(odd == 1, down))
+    crossed = jnp.logical_or(jnp.logical_and(even, down), jnp.logical_and(odd == 1, up))
+    from_slots = pl.ds(pl.multiple_of(128 + 64 * odd, 64), 64)
+    to_slots = pl.ds(pl.multiple_of(192 - 64 * odd, 64), 64)
+
+    @pl.when(jnp.logical_not(usable[1]))
     def _():
         received[2, 64:128, :] = jnp.zeros((64, 256), F32)
 
@@ -254,9 +239,25 @@
     def _():
         received[2, 0:64, :] = jnp.zeros((64, 256), F32)
 
-    sent[0] = outgoing
-    start(0, 1)
-    start(0, 0)
+    loads["border"].wait()
+    loads["halo"].wait()
+    loads["right"].wait()
+    loads["right_too"].wait()
+    field = right_ref[...]
+    field_cat = as_right(field)
+    for group in (1, 0):
+        for c in groups[group]:
+            tile = border_ref[0, c]
+            weights = halo_ref[0, c]
+            block = jnp.concatenate(
+                [jnp.where(tile == r, weights, jnp.zeros_like(weights)) for r in range(2)], axis=1
+            )
+            keep_left(halo_cat.at[64 * c : 64 * c + 64, :], block)
+        part = slice(128 * group, 128 * group + 128)
+        sent[0, part, :] = dot(halo_cat[part, :], field_cat)
+        if group:
+            pl.semaphore_wait(barrier, earlier + sum(u.astype(jnp.int32) for u in usable))
+        start(0, group)
 
     for bit, masks in partners_by_bit().items():
 
@@ -325,9 +326,9 @@
         if k == 0:
             ready = next_near - dependence * dot(hop_cat[0], first)
         else:
-            rows = jnp.concatenate([hop_cat[0, from_slots, :], hop_cat[0, 64:128, :]], axis=0)
-            crossing = jnp.where(even, next_near[192:256], next_near[128:192])
-            ready = jnp.concatenate([crossing, next_near[64:128]], axis=0)
+            rows = jnp.concatenate([hop_cat[0, from_slots, :], hop_cat[0, 0:64, :]], axis=0)
+            crossing = jnp.where(even, next_near[128:192], next_near[192:256])
+            ready = jnp.concatenate([crossing, next_near[0:64]], axis=0)
             ready = ready - dependence * dot(rows, first)
         finish(k, 1)
         second = as_right(dot(as_left(received[k, 128:256, :]), var_cat[...]))
@@ -337,10 +338,10 @@
                 sent[1, part, :] = ready[part] - dependence * dot(hop_cat[1, part, :], second)
                 start(1, group)
         else:
-            rows = jnp.concatenate([hop_cat[1, from_slots, :], hop_cat[1, 64:128, :]], axis=0)
+            rows = jnp.concatenate([hop_cat[1, from_slots, :], hop_cat[1, 0:64, :]], axis=0)
             sent[2, 0:128, :] = ready - dependence * dot(rows, second)
             pl.when(crosses)(last(1, me + across).start)
-            pl.when(usable[1])(last(0, me - 1).start)
+            pl.when(usable[0])(last(0, me + 1).start)
         image = image - dependence * dot(scatter[1], second[0:256])
         moments.append(fold(field * image))
         moments.append(fold(image * image))
@@ -351,7 +352,7 @@
     mapped = dot(as_left(field), var_cat[...])
     near = fold(dot(local_cat[...], field_cat) * mapped + noise * (field * field))
     high, low = split(mapped)
-    picks = jnp.concatenate([gather[to_slots, :], gather[0:64, :]], axis=0)
+    picks = jnp.concatenate([gather[to_slots, :], gather[64:128, :]], axis=0)
     picked = dot(picks, high) + dot(picks, low)
     picked = (-2.0 * dependence) * picked
     lane = lax.broadcasted_iota(jnp.int32, (8, 128), 1)
@@ -362,7 +363,10 @@
         return jnp.sum(jnp.where(lane == line_of, tile, 0.0), axis=0, keepdims=True)
 
     early = pack(moments + [near, jnp.zeros((2, 128), F32)])
-    pl.when(usable[0])(last(0, me + 1).wait_recv)
+    for k in range(2):
+        for c in range(4):
+            pl.when(usable[c])(copy(k, c, REVERSE[c]).wait_send)
+    pl.when(usable[1])(last(0, me - 1).wait_recv)
     pl.when(crossed)(last(1, me - across).wait_recv)
     cross = fold(picked * received[2, 0:128, :])
     later = sum(size - 1 for _, size in STAGES) - earlier
@@ -393,6 +397,10 @@
             device_id=(me,),
             device_id_type=MESH,
         )
+        if n == 1:
+            pl.when(usable[0])(last(0, me + 1).wait_send)
+            pl.when(crosses)(last(1, me + across).wait_send)
+            pending[0].wait_send()
         whole.wait_recv()
         total = jnp.sum(sums[...], axis=0, keepdims=True)
         pending.append(whole)
@@ -424,13 +432,7 @@
     c2 = a2 * f2
     out_ref[...] = c0 * basis[0] + c1 * basis[1] + c2 * basis[2]
 
-    for whole in pending:
-        whole.wait_send()
-    for k in range(2):
-        for c in range(4):
-            pl.when(usable[c])(copy(k, c, REVERSE[c]).wait_send)
-    pl.when(usable[1])(last(0, me - 1).wait_send)
-    pl.when(crosses)(last(1, me + across).wait_send)
+    pending[1].wait_send()
 
 
 def local(
@@ -496,7 +498,7 @@
             pltpu.VMEM((3, 256, 256), F32),
             pltpu.VMEM((STAGES[0][1], 128), F32),
             pltpu.VMEM((STAGES[1][1], 128), F32),
-            pltpu.SemaphoreType.DMA((11,)),
+            pltpu.SemaphoreType.DMA((12,)),
             pltpu.SemaphoreType.DMA((3, 4)),
             pltpu.SemaphoreType.DMA((3, 4)),
             pltpu.SemaphoreType.DMA((2,)),

time: 39.2 us -> 38.1 us (0.972)
  Pallas kernels: 37.7 us -> 36.5 us
    pallas_call x1, Pallas kernels: 37.7 us -> 36.5 us  [local(): pl.pallas_call(kernel, out_shape=pltpu.VMEM((256, 256), F32), in_specs=sp...]
where the time goes in v5:
time: 38.1 us; the launch traced here: 37.9 us
  Pallas kernels  36.5 us (96%)
  local copies, waits for them, and re-layouts  0.71 us (2%)
  between operations  0.66 us (2%)
    pallas_call x1, Pallas kernels, local(): pl.pallas_call(kernel, out_shape=pltpu.VMEM((256, 256), F32), in_specs=sp...  36.5 us

profile of v5, /device:TPU:1, one launch (start us, length us, event | category | flops | bytes accessed | tf_op | source)
XLA Modules:
  0.0 37.9 jit_solution(2157764352073042062)
XLA Ops:
  0.7 36.5 %conjugate_gradient.1 = f32[256,256]{1,0:T(8,128)S(1)} custom-call(f32[256,256]{1,0:T(8,128)} %right_hbm.1, bf16[256,256]{1,0:T(8,128)(2,1)} %noise_hbm.1, f32[1,256]{1,0:T(1,128)} %bitcast.3, f32[1]{0:T(128)} %bitcast.2.dependence_ref, f32[256,256]{1,0:T(8,128)} %var_hbm.1, f32[2,2,128,128]{3,2,1,0:T(8,128)} %tiles_hbm.1, s32[2,2]{1,0:T(2,128)} %cols_hbm.1, ...), custom_call_target="tpu_custom_call" | custom-call | tf_op jit(solution)/shard_map/conjugate_gradient/pallas_call | solution.py:483
  37.2 0.7 %copy.14 = f32[256,256]{1,0:T(8,128)} copy(f32[256,256]{1,0:T(8,128)S(1)} %conjugate_gradient.1) | data formatting | bytes 524288

commit v6 on v5

--- a/solution.py
+++ b/solution.py
@@ -185,13 +185,6 @@
     for name in ("var", "live", "rows", "tiles", "cols", "count", "degree", "noise"):
         loads[name].start()
 
-    for c in range(4):
-
-        @pl.when(jnp.logical_not(usable[c]))
-        def _():
-            for k in range(2):
-                received[k, 64 * c : 64 * c + 64, :] = jnp.zeros((64, 256), F32)
-
     def copy(k, c, to):
         return pltpu.make_async_remote_copy(
             src_ref=sent.at[k, 64 * c : 64 * c + 64, :],
@@ -259,14 +252,12 @@
             pl.semaphore_wait(barrier, earlier + sum(u.astype(jnp.int32) for u in usable))
         start(0, group)
 
-    for bit, masks in partners_by_bit().items():
-
-        @pl.when(jnp.bitwise_and(me, bit) != 0)
+    for c in range(4):
+
+        @pl.when(jnp.logical_not(usable[c]))
         def _():
-            for mask in masks:
-                answer = jnp.bitwise_xor(me, mask)
-                pl.semaphore_signal(answer_sem, inc=1, device_id=(answer,), device_id_type=MESH)
-
+            for k in range(2):
+                received[k, 64 * c : 64 * c + 64, :] = jnp.zeros((64, 256), F32)
 
     loads["var"].wait()
     keep_right(var_cat, var_ref[...])
@@ -314,6 +305,15 @@
         hop_cat[group, :, 128:256] = hop_high[:, part]
         hop_cat[group, :, 256:384] = hop_low[:, part]
     gather[...] = hot_wide.T.astype(BF16)
+
+    for bit, masks in partners_by_bit().items():
+
+        @pl.when(jnp.bitwise_and(me, bit) != 0)
+        def _():
+            for mask in masks:
+                answer = jnp.bitwise_xor(me, mask)
+                pl.semaphore_signal(answer_sem, inc=1, device_id=(answer,), device_id_type=MESH)
+
 
     basis[0] = field
     moments = [fold(field * field)]

time: 38.1 us -> 38.1 us (level)
  no operation moved by 1% of the time
where the time goes in v6:
time: 38.1 us; the launch traced here: 37.9 us
  Pallas kernels  36.5 us (96%)
  local copies, waits for them, and re-layouts  0.71 us (2%)
  between operations  0.66 us (2%)
    pallas_call x1, Pallas kernels, local(): pl.pallas_call(kernel, out_shape=pltpu.VMEM((256, 256), F32), in_specs=sp...  36.5 us

profile of v6, /device:TPU:1, one launch (start us, length us, event | category | flops | bytes accessed | tf_op | source)
XLA Modules:
  0.0 37.9 jit_solution(7277522247282965472)
XLA Ops:
  0.7 36.5 %conjugate_gradient.1 = f32[256,256]{1,0:T(8,128)S(1)} custom-call(f32[256,256]{1,0:T(8,128)} %right_hbm.1, bf16[256,256]{1,0:T(8,128)(2,1)} %noise_hbm.1, f32[1,256]{1,0:T(1,128)} %bitcast.3, f32[1]{0:T(128)} %bitcast.2.dependence_ref, f32[256,256]{1,0:T(8,128)} %var_hbm.1, f32[2,2,128,128]{3,2,1,0:T(8,128)} %tiles_hbm.1, s32[2,2]{1,0:T(2,128)} %cols_hbm.1, ...), custom_call_target="tpu_custom_call" | custom-call | tf_op jit(solution)/shard_map/conjugate_gradient/pallas_call | solution.py:483
  37.2 0.7 %copy.14 = f32[256,256]{1,0:T(8,128)} copy(f32[256,256]{1,0:T(8,128)S(1)} %conjugate_gradient.1) | data formatting | bytes 524288
